TPU v7x, 512 devices: a whole 4x4x16 slice. The times are simulated.
512 devices in a mesh: seq: 32 (over x, z_hi, core), chan: 16 (over y, z_lo).
Axes of the slice: x: 4, y: 4, z: 16 (z_hi: 4, z_lo: 4; z = z_hi * 4 + z_lo), core: 2. Of those that a mesh axis runs over, the one named last changes fastest.
Arguments:
- values: bfloat16 [4096, 16384], P('chan', 'seq'), may hold values from -6 to 6
- gates: bfloat16 [4096, 16384], P('chan', 'seq'), may hold values from -6 to 6
- skip_gain: float32 [4096], P('chan'), may hold values from 0.3 to 3
- filters: bfloat16 [4096, 16384], P('chan', 'seq'), may hold values from -6 to 6
- out_weight: bfloat16 [4096, 4096], P('seq', 'chan'), may hold values from -0.09375 to 0.09375
Outputs:
- projected: bfloat16 [4096, 16384], P('chan', 'seq')
All inputs are finite; a program needn't handle non-finite values.
Results may differ from a plain program's by a relative error of at most 0.0052.
Values may be sent and summed in bfloat16 or wider, within the bound.
A program may use at most 64 MiB of HBM per device.

v0:
```python
import functools

import jax
import jax.numpy as jnp
from jax import lax
from jax.experimental import pallas as pl
from jax.experimental.pallas import tpu as pltpu
from jax.sharding import PartitionSpec as P

MESH = pl.DeviceIdType.MESH
VMEM = pltpu.VMEM
BF16 = jnp.bfloat16
F32 = jnp.float32

NX, NZ, NC = 4, 4, 2
SEQ = NX * NZ * NC
NY, NL = 4, 4
LANES = 128
ROWS = 4
CH = 8


def mod(a, n):
    return lax.rem(a, n)


def seq_coords():
    s = lax.axis_index("seq")
    return s, lax.div(s, NZ * NC), mod(lax.div(s, NC), NZ), mod(s, NC)


def seq_id(x, z, c):
    return x * (NZ * NC) + z * NC + c


def signal(sem, seq, chan):
    pl.semaphore_signal(sem, inc=1, device_id={"seq": seq, "chan": chan}, device_id_type=MESH)


def remote(src, dst, ssem, rsem, seq, chan):
    return pltpu.make_async_remote_copy(
        src_ref=src, dst_ref=dst, send_sem=ssem, recv_sem=rsem,
        device_id={"seq": seq, "chan": chan}, device_id_type=MESH)


def scatter_kernel(v_ref, f_ref, got, out, ssem, rsem):
    me, x, z, c = seq_coords()
    chan = lax.axis_index("chan")
    barrier = pltpu.get_barrier_semaphore()

    def hello(k, _):
        signal(barrier, mod(me + k, SEQ), chan)
        return 0

    lax.fori_loop(1, SEQ, hello, 0)

    def pack(g, _):
        for ref, base in ((v_ref, 0), (f_ref, ROWS * CH)):
            block = ref[pl.ds(pl.multiple_of(16 * g, 16), 16), :].astype(F32)
            for half in range(2):
                part = block[CH * half:CH * (half + 1)]
                rows = [part[:, LANES * p:LANES * (p + 1)] for p in range(ROWS)]
                out[2 * g + half, base:base + ROWS * CH, :] = jnp.concatenate(rows, 0).astype(BF16)
        return 0

    lax.fori_loop(0, SEQ // 2, pack, 0)
    pl.semaphore_wait(barrier, SEQ - 1)

    def partner(dz, j, sign):
        dx, dc = lax.div(j, NC), mod(j, NC)
        return seq_id(mod(x + sign * dx + NX, NX), mod(z + sign * dz + NZ, NZ), mod(c + dc, NC))

    for dz in (2, 1, 3, 0):
        def send(j, _, dz=dz):
            to = partner(dz, j, 1)
            remote(out.at[to], got.at[me], ssem.at[to], rsem.at[me], to, chan).start()
            return 0

        lax.fori_loop(0 if dz else 1, NX * NC, send, 0)
    got[me] = out[me]
    for dz in (0, 1, 3, 2):
        def finish(j, _, dz=dz):
            to = partner(dz, j, 1)
            remote(out.at[to], got.at[to], ssem.at[to], rsem.at[to], to, chan).wait()
            return 0

        lax.fori_loop(0 if dz else 1, NX * NC, finish, 0)


def scatter(values, filters):
    return pl.pallas_call(
        scatter_kernel,
        out_shape=jax.ShapeDtypeStruct((SEQ, 2 * ROWS * CH, LANES), BF16),
        in_specs=[pl.BlockSpec(memory_space=VMEM)] * 2,
        out_specs=pl.BlockSpec(memory_space=VMEM),
        scratch_shapes=[
            VMEM((SEQ, 2 * ROWS * CH, LANES), BF16),
            pltpu.SemaphoreType.DMA((SEQ,)),
            pltpu.SemaphoreType.DMA((SEQ,)),
        ],
        compiler_params=pltpu.CompilerParams(
            collective_id=1, has_side_effects=True, vmem_limit_bytes=16 * 2**20),
        name="scatter_tokens",
    )(values, filters)


def conv_kernel(got_ref, y_ref, vf, ff, yf, lhs, rhs):
    count = SEQ * ROWS
    total_rows = count * CH
    vf[0:LANES, :] = jnp.zeros((LANES, LANES), F32)
    ff[0:CH, :] = jnp.zeros((CH, LANES), F32)
    half = ROWS * CH
    vf[LANES:, :] = got_ref[:, 0:half, :].astype(F32).reshape(total_rows, LANES)
    ff[CH:, :] = got_ref[:, half:, :].astype(F32).reshape(total_rows, LANES)
    row = lax.broadcasted_iota(jnp.int32, (LANES, LANES), 0)
    col = lax.broadcasted_iota(jnp.int32, (LANES, LANES), 1)
    keep = col >= row

    def turned(m, ch):
        line = ff[pl.ds(CH * m + CH + ch, 1), :]
        return pltpu.roll(jnp.broadcast_to(line, (LANES, LANES)), 0, 1, stride=1, stride_axis=0)

    def one(ch, _):
        for e in range(8):
            shifted = vf[pl.ds(LANES + ch - 16 * e, count, stride=CH), :]
            lhs[:, e * LANES:(e + 1) * LANES] = shifted.astype(BF16)
        before = turned(-1, ch)
        total = None
        for a in range(count // 16):
            for e in range(8):
                for odd in range(2):
                    now = turned(16 * a + 2 * e + odd, ch)
                    rhs[a % 2, e * LANES:(e + 1) * LANES, odd * LANES:(odd + 1) * LANES] = (
                        jnp.where(keep, now, before).astype(BF16))
                    before = now
            part = jnp.dot(lhs[0:count - 16 * a, :], rhs[a % 2], preferred_element_type=F32)
            if a:
                part = total + jnp.concatenate([jnp.zeros((16 * a, 2 * LANES), F32), part], 0)
            total = part
        yf[pl.ds(ch, count, stride=CH), :] = total[:, :LANES]
        yf[pl.ds(ch + CH, count - 1, stride=CH), :] += total[:count - 1, LANES:]
        return 0

    lax.fori_loop(0, CH, one, 0)
    y_ref[...] = yf[...].astype(BF16).reshape(SEQ, half, LANES)


def conv(got):
    count = SEQ * ROWS
    return pl.pallas_call(
        conv_kernel,
        out_shape=jax.ShapeDtypeStruct((SEQ, ROWS * CH, LANES), BF16),
        in_specs=[pl.BlockSpec(memory_space=VMEM)],
        out_specs=pl.BlockSpec(memory_space=VMEM),
        scratch_shapes=[
            VMEM((count * CH + LANES, LANES), F32),
            VMEM((count * CH + CH, LANES), F32),
            VMEM((count * CH, LANES), F32),
            VMEM((count, 8 * LANES), BF16),
            VMEM((2, 8 * LANES, 2 * LANES), BF16),
        ],
        compiler_params=pltpu.CompilerParams(vmem_limit_bytes=24 * 2**20),
        cost_estimate=pl.CostEstimate(
            flops=2 * CH * 2 * count * LANES * count * LANES, bytes_accessed=2**20, transcendentals=0),
        name="convolve",
    )(got)


def project_kernel(y_ref, v_ref, g_ref, skip_ref, w_ref, o_ref,
                   back, mix, weight, psend, pgot,
                   ssem, rsem, wssem, wrsem, mssem, mrsem, pssem, prsem):
    me, x, z, c = seq_coords()
    chan = lax.axis_index("chan")
    y, l = lax.div(chan, NL), mod(chan, NL)
    barrier = pltpu.get_barrier_semaphore()

    def hello(k, _):
        signal(barrier, mod(me + k, SEQ), chan)
        return 0

    lax.fori_loop(1, SEQ, hello, 0)
    for d in range(1, 4):
        signal(barrier, me, mod(y + d, NY) * NL + l)
        signal(barrier, me, y * NL + mod(l + d, NL))
    pl.semaphore_wait(barrier, SEQ - 1 + 6)

    def partner(dz, j):
        dx, dc = lax.div(j, NC), mod(j, NC)
        return seq_id(mod(x + dx, NX), mod(z + dz, NZ), mod(c + dc, NC))

    for dz in (2, 1, 3, 0):
        def send(j, _, dz=dz):
            to = partner(dz, j)
            remote(y_ref.at[to], back.at[me], ssem.at[to], rsem.at[me], to, chan).start()
            return 0

        lax.fori_loop(0 if dz else 1, NX * NC, send, 0)

    mine = x * NC + c

    def weight_copy(j, slot):
        dx, dc = lax.div(j, NC), mod(j, NC)
        to = seq_id(mod(x + dx, NX), z, mod(c + dc, NC))
        return remote(w_ref, weight.at[slot], wssem.at[j], wrsem.at[slot], to, chan)

    def send_weight(j, _):
        weight_copy(j, mine).start()
        return 0

    lax.fori_loop(1, NX * NC, send_weight, 0)
    weight[mine] = w_ref[...]
    back[me] = y_ref[me]

    def mix_copy(d, g, slot):
        rows = pl.ds(pl.multiple_of(16 * g, 16), 16)
        return remote(mix.at[slot, rows], mix.at[slot, rows], mssem.at[d - 1, g], mrsem.at[d - 1, g],
                      me, mod(y + d, NY) * NL + l)

    def blend(g):
        rows = pl.ds(pl.multiple_of(16 * g, 16), 16)
        first, second = back[2 * g].astype(F32), back[2 * g + 1].astype(F32)
        for p in range(ROWS):
            cols = slice(LANES * p, LANES * (p + 1))
            filtered = jnp.concatenate([first[CH * p:CH * (p + 1)], second[CH * p:CH * (p + 1)]], 0)
            value, gate = v_ref[rows, cols].astype(F32), g_ref[rows, cols].astype(F32)
            mix[y, rows, cols] = (gate * (filtered + skip_ref[rows, :] * value)).astype(BF16)
        for d in (2, 1, 3):
            mix_copy(d, g, y).start()

    def arrive(src):
        remote(y_ref.at[src], back.at[src], ssem.at[src], rsem.at[src], src, chan).wait()

    for dz in (0, 1, 3, 2):
        def step(dx, _, dz=dz):
            g = mod(x + dx, NX) * NZ + mod(z + dz, NZ)
            arrive(2 * g)
            arrive(2 * g + 1)
            blend(g)
            return 0

        if dz == 0:
            arrive(seq_id(x, z, 1 - c))
            blend(x * NZ + z)
        lax.fori_loop(0 if dz else 1, NX, step, 0)

    def weight_done(j, _):
        dx, dc = lax.div(j, NC), mod(j, NC)
        source = mod(x - dx + NX, NX) * NC + mod(c + dc, NC)
        weight_copy(j, source).wait()
        return 0

    lax.fori_loop(1, NX * NC, weight_done, 0)

    for d in (1, 3, 2):
        def mixed_done(g, _, d=d):
            mix_copy(d, g, mod(y - d + NY, NY)).wait()
            return 0

        lax.fori_loop(0, SEQ // 2, mixed_done, 0)

    def product(o):
        t = mod(z - o + NZ, NZ)
        left = jnp.concatenate([weight[j, t] for j in range(NX * NC)], 1)
        right = mix[...].reshape(NY * 2 * LANES, ROWS * LANES)
        return jnp.dot(left, right, preferred_element_type=F32)

    def partial_copy(d):
        return remote(psend.at[d - 1], pgot.at[d - 1], pssem.at[d - 1], prsem.at[d - 1],
                      me, y * NL + mod(l + d, NL))

    for d in (2, 1, 3):
        psend[d - 1] = product(mod(l + d, NL)).astype(BF16)
        partial_copy(d).start()
    total = product(l)
    for d in (1, 3, 2):
        partial_copy(d).wait()
    for d in (1, 3, 2):
        total = total + pgot[d - 1].astype(F32)
    o_ref[...] = total.astype(BF16)


def project(y, values, gates, skip, w):
    tokens = ROWS * LANES
    block = 2 * LANES
    return pl.pallas_call(
        project_kernel,
        out_shape=jax.ShapeDtypeStruct((block, tokens), BF16),
        in_specs=[pl.BlockSpec(memory_space=VMEM)] * 5,
        out_specs=pl.BlockSpec(memory_space=VMEM),
        scratch_shapes=[
            VMEM((SEQ, ROWS * CH, LANES), BF16),
            VMEM((NY, block, tokens), BF16),
            VMEM((NX * NC, NL, block, LANES), BF16),
            VMEM((3, block, tokens), BF16),
            VMEM((3, block, tokens), BF16),
            pltpu.SemaphoreType.DMA((SEQ,)),
            pltpu.SemaphoreType.DMA((SEQ,)),
            pltpu.SemaphoreType.DMA((NX * NC,)),
            pltpu.SemaphoreType.DMA((NX * NC,)),
            pltpu.SemaphoreType.DMA((3, SEQ // 2)),
            pltpu.SemaphoreType.DMA((3, SEQ // 2)),
            pltpu.SemaphoreType.DMA((3,)),
            pltpu.SemaphoreType.DMA((3,)),
        ],
        compiler_params=pltpu.CompilerParams(
            collective_id=2, has_side_effects=True, vmem_limit_bytes=32 * 2**20),
        name="mix_and_project",
    )(y, values, gates, skip, w)


def weight_route(turn):
    pairs = []
    for x in range(NX):
        for b in range(NZ):
            for c in range(NC):
                for y in range(NY):
                    for l in range(NL):
                        source = (x * NZ * NC + b * NC + c) * NY * NL + y * NL + l
                        target = (x * NZ * NC + (l + turn) % NZ * NC + c) * NY * NL + y * NL + b
                        pairs.append((source, target))
    return pairs


def per_device(values, gates, skip_gain, filters, out_weight):
    got = scatter(values, filters)
    turned = out_weight.T
    routed = jnp.stack([lax.ppermute(turned, ("seq", "chan"), weight_route(t)) for t in range(NZ)])
    y = conv(got)
    return project(y, values, gates, skip_gain[:, None], routed)


def solution(mesh):
    return jax.shard_map(
        per_device,
        mesh=mesh,
        in_specs=(
            P("chan", "seq"),
            P("chan", "seq"),
            P("chan"),
            P("chan", "seq"),
            P("seq", "chan"),
        ),
        out_specs=P("chan", "seq"),
        check_vma=False,
    )
```

profile of v0, /device:TPU:72, one launch (start us, length us, event | category | flops | bytes accessed | tf_op | source)
XLA Modules:
  0.0 144.0 jit_solution(910998458489743301)
XLA Ops:
  0.0 0.9 copy.7
  1.0 6.4 %collective-permute-start.3 = (bf16[256,128]{1,0:T(8,128)(2,1)S(1)}, bf16[256,128]{1,0:T(8,128)(2,1)S(1)}, u32[]{:S(2)}, u32[]{:S(2)}) collective-permute-start(bf16[256,128]{1,0:T(8,128)(2,1)S(1)} %bitcast.6), channel_id=1, source_target_pairs={{0,96},{1,0},{2,32},{3,64},{4,100},{5,4},{6,36},{7,68},{8,104},{9,... | collective-permute-start | bytes 196616 | tf_op jit(solution)/shard_map/ppermute | solution.py:327
  7.4 7.9 %collective-permute-start.2 = (bf16[256,128]{1,0:T(8,128)(2,1)S(1)}, bf16[256,128]{1,0:T(8,128)(2,1)S(1)}, u32[]{:S(2)}, u32[]{:S(2)}) collective-permute-start(bf16[256,128]{1,0:T(8,128)(2,1)S(1)} %bitcast.7), channel_id=1, source_target_pairs={{0,64},{1,96},{2,0},{3,32},{4,68},{5,100},{6,4},{7,36},{8,72},{9,1... | collective-permute-start | bytes 196616 | tf_op jit(solution)/shard_map/ppermute | solution.py:327
  15.3 4.6 %collective-permute-start.1 = (bf16[256,128]{1,0:T(8,128)(2,1)S(1)}, bf16[256,128]{1,0:T(8,128)(2,1)S(1)}, u32[]{:S(2)}, u32[]{:S(2)}) collective-permute-start(bf16[256,128]{1,0:T(8,128)(2,1)S(1)} %bitcast.8), channel_id=1, source_target_pairs={{0,32},{1,64},{2,96},{3,0},{4,36},{5,68},{6,100},{7,4},{8,40},{9,7... | collective-permute-start | bytes 196616 | tf_op jit(solution)/shard_map/ppermute | solution.py:327
  19.8 3.2 %collective-permute-start = (bf16[256,128]{1,0:T(8,128)(2,1)S(1)}, bf16[256,128]{1,0:T(8,128)(2,1)S(1)}, u32[]{:S(2)}, u32[]{:S(2)}) collective-permute-start(bf16[256,128]{1,0:T(8,128)(2,1)S(1)} %bitcast.9), channel_id=1, source_target_pairs={{0,0},{1,32},{2,64},{3,96},{4,4},{5,36},{6,68},{7,100},{8,8},{9,40... | collective-permute-start | bytes 196616 | tf_op jit(solution)/shard_map/ppermute | solution.py:327
  23.0 0.0 copy-start
  23.1 0.9 copy-done
  24.0 0.0 copy-start.2
  24.0 0.9 copy-done.2
  24.9 33.7 %scatter_tokens.1.got_ref = bf16[32,64,128]{2,1,0:T(8,128)(2,1)S(1)} custom-call(bf16[256,512]{1,0:T(8,128)(2,1)S(1)} %copy-done, bf16[256,512]{1,0:T(8,128)(2,1)S(1)} %copy-done.2), custom_call_target="tpu_custom_call" | custom-call | tf_op jit(solution)/shard_map/scatter_tokens/pallas_call | solution.py:91
  58.6 13.7 %convolve.1.y_ref = bf16[32,32,128]{2,1,0:T(8,128)(2,1)S(1)} custom-call(bf16[32,64,128]{2,1,0:T(8,128)(2,1)S(1)} %scatter_tokens.1.got_ref), custom_call_target="tpu_custom_call" | custom-call | flops 8589934592 | bytes 1048576 | tf_op jit(solution)/shard_map/convolve/pallas_call | solution.py:150
  72.4 0.0 copy-start.4
  72.4 0.7 copy-done.4
  73.0 0.1 copy.8.skip_ref
  73.2 0.0 collective-permute-done.3
  73.2 0.0 collective-permute-done.2
  73.2 0.0 collective-permute-done.1
  73.2 0.0 collective-permute-done
  73.2 0.0 copy-start.1
  73.2 0.0 copy-start.3
  73.3 0.9 copy-done.1
  74.2 0.1 copy-done.3
  74.3 69.0 %mix_and_project.1 = bf16[256,512]{1,0:T(8,128)(2,1)S(1)} custom-call(bf16[32,32,128]{2,1,0:T(8,128)(2,1)S(1)} %convolve.1.y_ref, bf16[256,512]{1,0:T(8,128)(2,1)S(1)} %copy-done.1, bf16[256,512]{1,0:T(8,128)(2,1)S(1)} %copy-done.3, f32[256,1]{1,0:T(8,128)S(1)} %copy.8.skip_ref, bf16[4,256,128]{2,1,0:T(8,128)(2,1)S(1)} %pad_maximum_fusion.w_ref), custom_call_target="tpu_custom_call" | custom-call | tf_op jit(solution)/shard_map/mix_and_project/pallas_call | solution.py:285
  143.3 0.7 copy.10
  (1 shorter events, 0.0 us)
Async XLA Ops:
  1.0 72.2 %collective-permute-start.3 = (bf16[256,128]{1,0:T(8,128)(2,1)S(1)}, bf16[256,128]{1,0:T(8,128)(2,1)S(1)}, u32[]{:S(2)}, u32[]{:S(2)}) collective-permute-start(bf16[256,128]{1,0:T(8,128)(2,1)S(1)} %bitcast.6), channel_id=1, source_target_pairs={{0,96},{1,0},{2,32},{3,64},{4,100},{5,4},{6,36},{7,68},{8,104},{9,... | collective-permute-start | bytes 196616 | tf_op jit(solution)/shard_map/ppermute | solution.py:327
  7.4 65.8 %collective-permute-start.2 = (bf16[256,128]{1,0:T(8,128)(2,1)S(1)}, bf16[256,128]{1,0:T(8,128)(2,1)S(1)}, u32[]{:S(2)}, u32[]{:S(2)}) collective-permute-start(bf16[256,128]{1,0:T(8,128)(2,1)S(1)} %bitcast.7), channel_id=1, source_target_pairs={{0,64},{1,96},{2,0},{3,32},{4,68},{5,100},{6,4},{7,36},{8,72},{9,1... | collective-permute-start | bytes 196616 | tf_op jit(solution)/shard_map/ppermute | solution.py:327
  15.3 57.9 %collective-permute-start.1 = (bf16[256,128]{1,0:T(8,128)(2,1)S(1)}, bf16[256,128]{1,0:T(8,128)(2,1)S(1)}, u32[]{:S(2)}, u32[]{:S(2)}) collective-permute-start(bf16[256,128]{1,0:T(8,128)(2,1)S(1)} %bitcast.8), channel_id=1, source_target_pairs={{0,32},{1,64},{2,96},{3,0},{4,36},{5,68},{6,100},{7,4},{8,40},{9,7... | collective-permute-start | bytes 196616 | tf_op jit(solution)/shard_map/ppermute | solution.py:327
  19.8 53.4 %collective-permute-start = (bf16[256,128]{1,0:T(8,128)(2,1)S(1)}, bf16[256,128]{1,0:T(8,128)(2,1)S(1)}, u32[]{:S(2)}, u32[]{:S(2)}) collective-permute-start(bf16[256,128]{1,0:T(8,128)(2,1)S(1)} %bitcast.9), channel_id=1, source_target_pairs={{0,0},{1,32},{2,64},{3,96},{4,4},{5,36},{6,68},{7,100},{8,8},{9,40... | collective-permute-start | bytes 196616 | tf_op jit(solution)/shard_map/ppermute | solution.py:327
  23.0 1.0 copy-start
  24.0 0.9 copy-start.2
  72.4 0.7 copy-start.4
  73.2 1.0 copy-start.1
  73.2 1.0 copy-start.3
where the time goes:
time: 144 us
  Pallas kernels  116 us (81%)
  starting transfers between devices  22.1 us (15%)
  local copies, waits for them, and re-layouts  5.33 us (4%)
    pallas_call x1, Pallas kernels, project(): pl.pallas_call(project_kernel, out_shape=jax.ShapeDtypeStruct((block, tok...  69 us
    pallas_call x1, Pallas kernels, scatter(): pl.pallas_call(scatter_kernel, out_shape=jax.ShapeDtypeStruct((SEQ, 2 * R...  33.7 us
    ppermute x4, starting transfers between devices, per_device(): lax.ppermute(turned, ('seq', 'chan'), weight_route(t))  22.1 us
    pallas_call x1, Pallas kernels, conv(): pl.pallas_call(conv_kernel, out_shape=jax.ShapeDtypeStruct((SEQ, ROWS * C...  13.7 us
    unnamed x12, local copies, waits for them, and re-layouts  5.2 us
  transfers between devices with their start and end apart: 4, of which 0 were waited for; matrix products, arithmetic and copies ran while one was open for 0% of the time, Pallas kernels for 33%

commit v1 on v0

v1 whole, which is shorter than its diff:
```python
import functools

import jax
import jax.numpy as jnp
from jax import lax
from jax.experimental import pallas as pl
from jax.experimental.pallas import tpu as pltpu
from jax.sharding import PartitionSpec as P

MESH = pl.DeviceIdType.MESH
VMEM = pltpu.VMEM
BF16 = jnp.bfloat16
F32 = jnp.float32

NX, NZ, NC = 4, 4, 2
SEQ = NX * NZ * NC
NY, NL = 4, 4
LANES = 128
ROWS = 4
PARTS = 2
CH = 4
TOKENS = ROWS * LANES
BLOCK = PARTS * CH * SEQ
COUNT = SEQ * ROWS
BOX = ROWS * CH


def mod(a, n):
    return lax.rem(a, n)


def seq_coords():
    s = lax.axis_index("seq")
    return s, lax.div(s, NZ * NC), mod(lax.div(s, NC), NZ), mod(s, NC)


def seq_id(x, z, c):
    return x * (NZ * NC) + z * NC + c


def signal(sem, seq, chan):
    pl.semaphore_signal(sem, inc=1, device_id={"seq": seq, "chan": chan}, device_id_type=MESH)


def remote(src, dst, ssem, rsem, seq, chan):
    return pltpu.make_async_remote_copy(
        src_ref=src, dst_ref=dst, send_sem=ssem, recv_sem=rsem,
        device_id={"seq": seq, "chan": chan}, device_id_type=MESH)


def halves(x, y):
    low = lax.broadcasted_iota(jnp.int32, (8, LANES), 0) < CH
    return jnp.where(low, x, pltpu.roll(y, CH, 0)), jnp.where(low, pltpu.roll(x, CH, 0), y)


def convolve(load, vf, ff, yf, lhs, rhs):
    vf[0:LANES, :] = jnp.zeros((LANES, LANES), F32)
    ff[0:CH, :] = jnp.zeros((CH, LANES), F32)
    load()
    row = lax.broadcasted_iota(jnp.int32, (LANES, LANES), 0)
    col = lax.broadcasted_iota(jnp.int32, (LANES, LANES), 1)
    keep = col >= row

    def turned(m, ch):
        line = ff[pl.ds(CH * m + CH + ch, 1), :]
        return pltpu.roll(jnp.broadcast_to(line, (LANES, LANES)), 0, 1, stride=1, stride_axis=0)

    def one(ch, _):
        for e in range(8):
            shifted = vf[pl.ds(LANES + ch - 2 * CH * e, COUNT, stride=CH), :]
            lhs[:, e * LANES:(e + 1) * LANES] = shifted.astype(BF16)
        before = turned(-1, ch)
        total = None
        for a in range(COUNT // 16):
            for e in range(8):
                for odd in range(2):
                    now = turned(16 * a + 2 * e + odd, ch)
                    rhs[a % 2, e * LANES:(e + 1) * LANES, odd * LANES:(odd + 1) * LANES] = (
                        jnp.where(keep, now, before).astype(BF16))
                    before = now
            part = jnp.dot(lhs[0:COUNT - 16 * a, :], rhs[a % 2], preferred_element_type=F32)
            if a:
                part = total + jnp.concatenate([jnp.zeros((16 * a, 2 * LANES), F32), part], 0)
            total = part
        yf[pl.ds(ch, COUNT, stride=CH), :] = total[:, :LANES]
        yf[pl.ds(ch + CH, COUNT - 1, stride=CH), :] += total[:COUNT - 1, LANES:]
        return 0

    lax.fori_loop(0, CH, one, 0)


def block_kernel(v_hbm, f_hbm, g_hbm, skip_ref, w_hbm, o_ref,
                 v_ref, f_ref, g_ref, w_ref, out, got, vf, ff, yf, lhs, rhs, done, back, mix, wt, weight,
                 psend, pgot, lsem, ssem, rsem, bssem, brsem, w1s, w1r, w2s, w2r, w3s, w3r,
                 mssem, mrsem, pssem, prsem):
    me, x, z, c = seq_coords()
    chan = lax.axis_index("chan")
    y, l = lax.div(chan, NL), mod(chan, NL)
    barrier = pltpu.get_barrier_semaphore()

    local = [pltpu.make_async_copy(a, b, lsem.at[i])
             for i, (a, b) in enumerate(((v_hbm, v_ref), (f_hbm, f_ref), (w_hbm, w_ref), (g_hbm, g_ref)))]
    for copy in local:
        copy.start()

    def hello(k, _):
        signal(barrier, mod(me + k, SEQ), chan)
        return 0

    lax.fori_loop(1, SEQ, hello, 0)
    for d in range(1, 4):
        signal(barrier, me, mod(y + d, NY) * NL + l)
        signal(barrier, me, y * NL + mod(l + d, NL))
    for t in range(1, NZ):
        signal(barrier, seq_id(x, l, c), y * NL + mod(z - t + NZ, NZ))

    @pl.when(l != z)
    def _():
        signal(barrier, seq_id(x, l, c), y * NL + z)

    def partner(dz, j):
        dx, dc = lax.div(j, NC), mod(j, NC)
        return seq_id(mod(x + dx, NX), mod(z + dz, NZ), mod(c + dc, NC))

    def each_partner(body, order=(2, 1, 3, 0)):
        for dz in order:
            def step(j, _, dz=dz):
                body(partner(dz, j))
                return 0

            lax.fori_loop(0 if dz else 1, NX * NC, step, 0)

    def pack(q):
        def step(h, _):
            rows = pl.ds(pl.multiple_of(BLOCK // PARTS * q + 16 * h, 16), 16)
            for ref, base in ((v_ref, 0), (f_ref, BOX)):
                block = ref[rows, :].astype(F32)
                for u in range(2):
                    p = [block[8 * u:8 * u + 8, LANES * i:LANES * (i + 1)] for i in range(ROWS)]
                    first, second = halves(p[0], p[1]), halves(p[2], p[3])
                    for odd in range(2):
                        out[q, 4 * h + 2 * u + odd, base:base + BOX, :] = jnp.concatenate(
                            [first[odd], second[odd]], 0).astype(BF16)
            return 0

        lax.fori_loop(0, SEQ // 4, step, 0)

    def scatter_copy(q, to, slot):
        return remote(out.at[q, to], got.at[q, slot], ssem.at[q, to], rsem.at[q, slot], to, chan)

    def return_copy(q, to, slot):
        return remote(done.at[q, to], back.at[q, slot], bssem.at[q, to], brsem.at[q, slot], to, chan)

    local[0].wait()
    local[1].wait()
    pack(0)
    pl.semaphore_wait(barrier, SEQ - 1 + 6 + 3 + jnp.where(l == z, 0, 1))
    each_partner(lambda to: scatter_copy(0, to, me).start())
    pack(1)
    each_partner(lambda to: scatter_copy(1, to, me).start())
    got[0, me] = out[0, me]
    got[1, me] = out[1, me]
    local[2].wait()
    wt[...] = w_ref[...].astype(F32).T.astype(BF16)
    local[3].wait()

    mine = x * NC + c

    def weight_copy(t):
        return remote(wt, weight.at[mine, t], w1s.at[t], w1r.at[t],
                      seq_id(x, mod(l + t, NZ), c), y * NL + z)

    for q in range(PARTS):
        each_partner(lambda to: scatter_copy(q, to, to).wait_recv())
        if q == 0:
            for t in range(1, NZ):
                weight_copy(t).start()

            @pl.when(l != z)
            def _():
                weight_copy(0).start()

            @pl.when(l == z)
            def _():
                weight[mine, 0] = wt[...]

        def load(q=q):
            vf[LANES:, :] = got[q, :, 0:BOX, :].astype(F32).reshape(COUNT * CH, LANES)
            ff[CH:, :] = got[q, :, BOX:, :].astype(F32).reshape(COUNT * CH, LANES)

        convolve(load, vf, ff, yf, lhs, rhs)
        done[q] = yf[...].astype(BF16).reshape(SEQ, BOX, LANES)
        each_partner(lambda to: return_copy(q, to, me).start())
        back[q, me] = done[q, me]

    for t in range(1, NZ):
        weight_copy(t).wait()

    @pl.when(l != z)
    def _():
        weight_copy(0).wait()

    def across_copy(d, slot):
        return remote(weight.at[slot], weight.at[slot], w2s.at[d - 1], w2r.at[d - 1],
                      seq_id(mod(x + d, NX), z, c), chan)

    def core_copy(d, slot):
        return remote(weight.at[slot], weight.at[slot], w3s.at[d], w3r.at[d], seq_id(x, z, 1 - c), chan)

    for d in (2, 1, 3):
        across_copy(d, mine).start()
    core_copy(0, mine).start()

    def mix_copy(d, b, slot):
        rows = pl.ds(pl.multiple_of(16 * b, 16), 16)
        return remote(mix.at[slot, rows], mix.at[slot, rows], mssem.at[d - 1, b], mrsem.at[d - 1, b],
                      me, mod(y + d, NY) * NL + l)

    def blend(q, h):
        start = pl.multiple_of(BLOCK // PARTS * q + 16 * h, 16)
        rows = pl.ds(start, 16)
        filtered = [[], [], [], []]
        for u in range(2):
            even, odd = back[q, 4 * h + 2 * u].astype(F32), back[q, 4 * h + 2 * u + 1].astype(F32)
            for i in range(2):
                pair = halves(even[8 * i:8 * i + 8], odd[8 * i:8 * i + 8])
                filtered[2 * i].append(pair[0])
                filtered[2 * i + 1].append(pair[1])
        for i in range(ROWS):
            cols = slice(LANES * i, LANES * (i + 1))
            value, gate = v_ref[rows, cols].astype(F32), g_ref[rows, cols].astype(F32)
            total = jnp.concatenate(filtered[i], 0) + skip_ref[rows, :] * value
            mix[y, rows, cols] = (gate * total).astype(BF16)
        for d in (2, 1, 3):
            mix_copy(d, (SEQ // 4) * q + h, y).start()

    for q in range(PARTS):
        for dz in range(2):
            def step(dx, _, dz=dz, q=q):
                h = mod(x + dx, NX) * 2 + mod(lax.div(z, 2) + dz, 2)
                for i in range(4):
                    src = 4 * h + i

                    @pl.when(src != me)
                    def _():
                        return_copy(q, src, src).wait_recv()

                blend(q, h)
                return 0

            lax.fori_loop(0, NX, step, 0)
        if q == 0:
            for d in (1, 3, 2):
                slot = mod(x - d + NX, NX) * NC + c
                across_copy(d, slot).wait()
                core_copy(d, slot).start()

    for d in range(NX):
        core_copy(d, mod(x - d + NX, NX) * NC + 1 - c).wait()

    for d in (1, 3, 2):
        def mixed_done(b, _, d=d):
            mix_copy(d, b, mod(y - d + NY, NY)).wait()
            return 0

        lax.fori_loop(0, BLOCK // 16, mixed_done, 0)

    def product(o):
        t = mod(z - o + NZ, NZ)
        left = jnp.concatenate([weight[j, t] for j in range(NX * NC)], 1)
        right = mix[...].reshape(NY * BLOCK, TOKENS)
        return jnp.dot(left, right, preferred_element_type=F32)

    def partial_copy(d):
        return remote(psend.at[d - 1], pgot.at[d - 1], pssem.at[d - 1], prsem.at[d - 1],
                      me, y * NL + mod(l + d, NL))

    for d in (2, 1, 3):
        psend[d - 1] = product(mod(l + d, NL)).astype(BF16)
        partial_copy(d).start()
    total = product(l)
    for q in range(PARTS):
        each_partner(lambda to: scatter_copy(q, to, me).wait_send())
        each_partner(lambda to: return_copy(q, to, me).wait_send())
    for d in (1, 3, 2):
        partial_copy(d).wait()
    for d in (1, 3, 2):
        total = total + pgot[d - 1].astype(F32)
    o_ref[...] = total.astype(BF16)


def per_device(values, gates, skip_gain, filters, out_weight):
    dma = pltpu.SemaphoreType.DMA
    hbm = pl.BlockSpec(memory_space=pl.ANY)
    vmem = pl.BlockSpec(memory_space=VMEM)
    return pl.pallas_call(
        block_kernel,
        out_shape=jax.ShapeDtypeStruct((BLOCK, TOKENS), BF16),
        in_specs=[hbm, hbm, hbm, vmem, hbm],
        out_specs=vmem,
        scratch_shapes=[
            VMEM((BLOCK, TOKENS), BF16), VMEM((BLOCK, TOKENS), BF16), VMEM((BLOCK, TOKENS), BF16),
            VMEM((LANES, BLOCK), BF16),
            VMEM((PARTS, SEQ, 2 * BOX, LANES), BF16), VMEM((PARTS, SEQ, 2 * BOX, LANES), BF16),
            VMEM((COUNT * CH + LANES, LANES), F32), VMEM((COUNT * CH + CH, LANES), F32),
            VMEM((COUNT * CH, LANES), F32),
            VMEM((COUNT, 8 * LANES), BF16), VMEM((2, 8 * LANES, 2 * LANES), BF16),
            VMEM((PARTS, SEQ, BOX, LANES), BF16), VMEM((PARTS, SEQ, BOX, LANES), BF16),
            VMEM((NY, BLOCK, TOKENS), BF16),
            VMEM((BLOCK, LANES), BF16), VMEM((NX * NC, NL, BLOCK, LANES), BF16),
            VMEM((3, BLOCK, TOKENS), BF16), VMEM((3, BLOCK, TOKENS), BF16),
            dma((4,)), dma((PARTS, SEQ)), dma((PARTS, SEQ)), dma((PARTS, SEQ)), dma((PARTS, SEQ)),
            dma((NZ,)), dma((NZ,)), dma((3,)), dma((3,)), dma((NX,)), dma((NX,)),
            dma((3, BLOCK // 16)), dma((3, BLOCK // 16)), dma((3,)), dma((3,)),
        ],
        compiler_params=pltpu.CompilerParams(
            collective_id=1, has_side_effects=True, vmem_limit_bytes=40 * 2**20),
        name="hyena_block",
    )(values, filters, gates, skip_gain[:, None], out_weight)


def solution(mesh):
    return jax.shard_map(
        per_device,
        mesh=mesh,
        in_specs=(
            P("chan", "seq"),
            P("chan", "seq"),
            P("chan"),
            P("chan", "seq"),
            P("seq", "chan"),
        ),
        out_specs=P("chan", "seq"),
        check_vma=False,
    )
```

time: 144 us -> 121 us (0.84)
  the two profiles are of different devices: /device:TPU:72 before, /device:TPU:33 now
where the time goes in v1:
time: 121 us; the launch traced here: 120 us
  Pallas kernels  115 us (95%)
  local copies, waits for them, and re-layouts  5.06 us (4%)
    pallas_call x1, Pallas kernels, per_device(): pl.pallas_call(block_kernel, out_shape=jax.ShapeDtypeStruct((BLOCK, TOKEN...  115 us
    unnamed x11, local copies, waits for them, and re-layouts  4.93 us

profile of v1, /device:TPU:33, one launch (start us, length us, event | category | flops | bytes accessed | tf_op | source)
XLA Modules:
  0.0 120.3 jit_solution(11540206376583021811)
XLA Ops:
  0.0 0.0 copy-start.4
  0.0 0.7 copy-done.4
  0.7 0.0 copy-start.3
  0.7 0.1 copy.6.skip_ref
  0.8 0.7 copy-done.3
  1.5 0.0 copy-start
  1.5 0.9 copy-done
  2.5 0.0 copy-start.1
  2.5 0.9 copy-done.1
  3.4 0.0 copy-start.2
  3.4 0.9 copy-done.2
  4.4 115.2 %hyena_block.1 = bf16[256,512]{1,0:T(8,128)(2,1)S(1)} custom-call(bf16[256,512]{1,0:T(8,128)(2,1)S(1)} %copy-done, bf16[256,512]{1,0:T(8,128)(2,1)S(1)} %copy-done.1, bf16[256,512]{1,0:T(8,128)(2,1)S(1)} %copy-done.2, f32[256,1]{1,0:T(8,128)S(1)} %copy.6.skip_ref, bf16[128,256]{1,0:T(8,128)(2,1)S(1)} %copy-done.3), custom_call_target="tpu_custom_call" | custom-call | tf_op jit(solution)/shard_map/hyena_block/pallas_call | solution.py:296
  119.6 0.7 copy.8
Async XLA Ops:
  0.0 0.7 copy-start.4
  0.7 0.8 copy-start.3
  1.5 0.9 copy-start
  2.5 0.9 copy-start.1
  3.4 0.9 copy-start.2

commit v2 on v1

v2 whole, which is shorter than its diff:
```python
import functools

import jax
import jax.numpy as jnp
from jax import lax
from jax.experimental import pallas as pl
from jax.experimental.pallas import tpu as pltpu
from jax.sharding import PartitionSpec as P

MESH = pl.DeviceIdType.MESH
VMEM = pltpu.VMEM
BF16 = jnp.bfloat16
F32 = jnp.float32

NX, NZ, NC = 4, 4, 2
SEQ = NX * NZ * NC
NY, NL = 4, 4
LANES = 128
ROWS = 4
PARTS = 2
CH = 4
TOKENS = ROWS * LANES
BLOCK = PARTS * CH * SEQ
COUNT = SEQ * ROWS
BOX = ROWS * CH


def mod(a, n):
    return lax.rem(a, n)


def seq_coords():
    s = lax.axis_index("seq")
    return s, lax.div(s, NZ * NC), mod(lax.div(s, NC), NZ), mod(s, NC)


def seq_id(x, z, c):
    return x * (NZ * NC) + z * NC + c


def signal(sem, seq, chan):
    pl.semaphore_signal(sem, inc=1, device_id={"seq": seq, "chan": chan}, device_id_type=MESH)


def remote(src, dst, ssem, rsem, seq, chan):
    return pltpu.make_async_remote_copy(
        src_ref=src, dst_ref=dst, send_sem=ssem, recv_sem=rsem,
        device_id={"seq": seq, "chan": chan}, device_id_type=MESH)


def halves(x, y):
    low = lax.broadcasted_iota(jnp.int32, (8, LANES), 0) < CH
    return jnp.where(low, x, pltpu.roll(y, CH, 0)), jnp.where(low, pltpu.roll(x, CH, 0), y)


def convolve(load, vf, ff, yf, lhs, rhs, acc):
    vf[0:LANES, :] = jnp.zeros((LANES, LANES), F32)
    ff[0:CH, :] = jnp.zeros((CH, LANES), F32)
    load()
    half = LANES // 2
    row = lax.broadcasted_iota(jnp.int32, (half, LANES), 0)
    col = lax.broadcasted_iota(jnp.int32, (half, LANES), 1)
    keep = col >= row
    low = lax.broadcasted_iota(jnp.int32, (COUNT, LANES), 1) < half

    def turned(m, ch):
        line = ff[pl.ds(CH * m + CH + ch, 1), :]
        return pltpu.roll(jnp.broadcast_to(line, (half, LANES)), 0, 1, stride=1, stride_axis=0)

    def one(ch, _):
        for e in range(0, 8, 2):
            a, b = (vf[pl.ds(LANES + ch - 2 * CH * i, COUNT, stride=CH), :] for i in (e, e + 1))
            cols = slice(e * half, (e + 2) * half)
            lhs[0, :, cols] = jnp.where(low, a, pltpu.roll(b, half, 1)).astype(BF16)
            lhs[1, :, cols] = jnp.where(low, pltpu.roll(a, half, 1), b).astype(BF16)
        before = turned(-1, ch)
        for a in range(COUNT // 16):
            for e in range(8):
                for odd in range(2):
                    now = turned(16 * a + 2 * e + odd, ch)
                    rhs[a % 2, e * half:(e + 1) * half, odd * LANES:(odd + 1) * LANES] = (
                        jnp.where(keep, now, before).astype(BF16))
                    before = now
            rows = COUNT - 16 * a
            left = lhs[:, 0:rows, :].reshape(2 * rows, 8 * half)
            part = jnp.dot(left, rhs[a % 2], preferred_element_type=F32).reshape(2, rows, 2 * LANES)
            if a:
                acc[:, 16 * a:, :] += part
            else:
                acc[...] = part
        first, second = pltpu.roll(acc[1, :, :LANES], half, 1), pltpu.roll(acc[1, :, LANES:], half, 1)
        yf[pl.ds(ch, COUNT, stride=CH), :] = acc[0, :, :LANES] + jnp.where(low, 0.0, first)
        later = acc[0, :, LANES:] + jnp.where(low, first, second)
        yf[pl.ds(ch + CH, COUNT - 1, stride=CH), :] += later[:COUNT - 1]
        yf[pl.ds(ch + 2 * CH, COUNT - 2, stride=CH), :] += jnp.where(low, second, 0.0)[:COUNT - 2]
        return 0

    lax.fori_loop(0, CH, one, 0)


def block_kernel(v_hbm, f_hbm, g_hbm, s_hbm, w_hbm, o_ref,
                 v_ref, f_ref, g_ref, s_ref, w_ref, skip, out, got, vf, ff, yf, lhs, rhs, cacc, done, back, mix, early, weight,
                 acc, psend, pgot, lsem, ssem, rsem, bssem, brsem, w1s, w1r, w2s, w2r, w3s, w3r,
                 mssem, mrsem, cssem, crsem, pssem, prsem):
    me, x, z, c = seq_coords()
    chan = lax.axis_index("chan")
    y, l = lax.div(chan, NL), mod(chan, NL)
    barrier = pltpu.get_barrier_semaphore()

    local = [pltpu.make_async_copy(a, b, lsem.at[i])
             for i, (a, b) in enumerate(((v_hbm, v_ref), (f_hbm, f_ref), (w_hbm, w_ref), (g_hbm, g_ref), (s_hbm, s_ref)))]
    for copy in local:
        copy.start()

    def hello(k, _):
        signal(barrier, mod(me + k, SEQ), chan)
        return 0

    lax.fori_loop(1, SEQ, hello, 0)
    for d in range(1, 4):
        signal(barrier, me, mod(y + d, NY) * NL + l)
        signal(barrier, me, y * NL + mod(l + d, NL))
    for t in range(1, NX):
        signal(barrier, seq_id(y, z, c), mod(x - t + NX, NX) * NL + l)

    @pl.when(x != y)
    def _():
        signal(barrier, seq_id(y, z, c), x * NL + l)

    def partner(dz, j):
        dx, dc = lax.div(j, NC), mod(j, NC)
        return seq_id(mod(x + dx, NX), mod(z + dz, NZ), mod(c + dc, NC))

    def each_partner(body, order=(2, 1, 3, 0)):
        for dz in order:
            def step(j, _, dz=dz):
                body(partner(dz, j))
                return 0

            lax.fori_loop(0 if dz else 1, NX * NC, step, 0)

    def pack(q):
        def step(h, _):
            rows = pl.ds(pl.multiple_of(BLOCK // PARTS * q + 16 * h, 16), 16)
            for ref, base in ((v_ref, 0), (f_ref, BOX)):
                block = ref[rows, :].astype(F32)
                for u in range(2):
                    p = [block[8 * u:8 * u + 8, LANES * i:LANES * (i + 1)] for i in range(ROWS)]
                    first, second = halves(p[0], p[1]), halves(p[2], p[3])
                    for odd in range(2):
                        out[q, 4 * h + 2 * u + odd, base:base + BOX, :] = jnp.concatenate(
                            [first[odd], second[odd]], 0).astype(BF16)
            return 0

        lax.fori_loop(0, SEQ // 4, step, 0)

    def scatter_copy(q, to, slot):
        return remote(out.at[q, to], got.at[q, slot], ssem.at[q, to], rsem.at[q, slot], to, chan)

    def return_copy(q, to, slot):
        return remote(done.at[q, to], back.at[q, slot], bssem.at[q, to], brsem.at[q, slot], to, chan)

    local[0].wait()
    local[1].wait()
    pack(0)
    local[2].wait()
    early[z] = w_ref[...].astype(F32).T.astype(BF16)

    def weight_copy(i, slot):
        ref = early.at[slot] if i < 2 else early.at[slot, pl.ds(LANES * (i - 2), LANES)]
        return remote(ref, ref, w1s.at[i], w1r.at[i], seq_id(x, mod(z + (3 if i % 2 else 1), NZ), c), chan)

    def across_copy(b, t):
        return remote(early.at[b], weight.at[c, t, b], w2s.at[b, t], w2r.at[b, t],
                      seq_id(mod(y + t, NX), z, c), x * NL + l)

    def send_across(b):
        for t in range(1, NX):
            across_copy(b, t).start()

        @pl.when(x != y)
        def _():
            across_copy(b, 0).start()

        @pl.when(x == y)
        def _():
            weight[c, 0, b] = early[b]

    def relay_weights():
        for i, slot in ((0, mod(z + 3, NZ)), (1, mod(z + 1, NZ))):
            weight_copy(i, slot).wait()
            weight_copy(2 + i, slot).start()
            send_across(slot)

    def finish_weights():
        slot = mod(z + 2, NZ)
        weight_copy(2, slot).wait()
        weight_copy(3, slot).wait()
        send_across(slot)

    def share_weights():
        for b in range(NZ):
            for t in range(1, NX):
                across_copy(b, t).wait()

            @pl.when(x != y)
            def _():
                across_copy(b, 0).wait()

        for t in range(NX):
            core_copy(t, c).start()

    def core_copy(t, half):
        return remote(weight.at[half, t], weight.at[half, t], w3s.at[t], w3r.at[t],
                      seq_id(x, z, 1 - c), chan)

    pl.semaphore_wait(barrier, SEQ - 1 + 6 + 3 + jnp.where(x == y, 0, 1))
    each_partner(lambda to: scatter_copy(0, to, me).start())
    pack(1)
    each_partner(lambda to: scatter_copy(1, to, me).start())
    weight_copy(0, z).start()
    weight_copy(1, z).start()
    send_across(z)
    got[0, me] = out[0, me]
    got[1, me] = out[1, me]
    local[3].wait()
    local[4].wait()
    for q in range(BLOCK // LANES):
        line = s_ref[:, LANES * q:LANES * (q + 1)]
        skip[LANES * q:LANES * (q + 1), :] = jnp.broadcast_to(line, (LANES, LANES)).T

    for q in range(PARTS):
        each_partner(lambda to: scatter_copy(q, to, to).wait_recv())
        if q == 0:
            relay_weights()

        def load(q=q):
            vf[LANES:, :] = got[q, :, 0:BOX, :].astype(F32).reshape(COUNT * CH, LANES)
            ff[CH:, :] = got[q, :, BOX:, :].astype(F32).reshape(COUNT * CH, LANES)

        convolve(load, vf, ff, yf, lhs, rhs, cacc)
        done[q] = yf[...].astype(BF16).reshape(SEQ, BOX, LANES)
        each_partner(lambda to: return_copy(q, to, me).start())
        back[q, me] = done[q, me]

    pieces = ((0, 0, ROWS), (1, 0, ROWS // 2), (1, ROWS // 2, ROWS))

    def piece_at(k, h):
        q, first, last = pieces[k]
        rows = pl.ds(pl.multiple_of(BLOCK // PARTS * q + 16 * h, 16), 16)
        return rows, slice(LANES * first, LANES * last)

    def mix_copy(d, k, h, slot):
        ref = mix.at[(slot,) + piece_at(k, h)]
        b = SEQ // 4 * (k - 1) + h
        return remote(ref, ref, mssem.at[d - 1, b], mrsem.at[d - 1, b], me, y * NL + mod(l + d, NL))

    def blend(k, h):
        q, first, last = pieces[k]
        rows, _ = piece_at(k, h)
        filtered = [[], [], [], []]
        for u in range(2):
            even, odd = back[q, 4 * h + 2 * u].astype(F32), back[q, 4 * h + 2 * u + 1].astype(F32)
            for i in range(first // 2, last // 2):
                pair = halves(even[8 * i:8 * i + 8], odd[8 * i:8 * i + 8])
                filtered[2 * i].append(pair[0])
                filtered[2 * i + 1].append(pair[1])
        for i in range(first, last):
            cols = slice(LANES * i, LANES * (i + 1))
            value, gate = v_ref[rows, cols].astype(F32), g_ref[rows, cols].astype(F32)
            total = jnp.concatenate(filtered[i], 0) + skip[rows, :] * value
            mix[l, rows, cols] = (gate * total).astype(BF16)
        if k:
            for d in (2, 1, 3):
                mix_copy(d, k, h, l).start()

    def chain_copy(slot, way):
        ref = mix.at[slot, pl.ds(0, BLOCK // PARTS)]
        return remote(ref, ref, cssem.at[slot, way], crsem.at[slot], me,
                      y * NL + mod(l + (3 if way else 1), NL))

    def on_chain(j, body):
        @pl.when(l >= j)
        def _():
            body(mod(l - j + NL, NL), 0)

        @pl.when(l < NL - j)
        def _():
            body(mod(l + j, NL), 1)

    def pass_on(slot, way):
        @pl.when(l > 0 if way else l < NL - 1)
        def _():
            chain_copy(slot, way).start()

    def relay(slot, way):
        chain_copy(slot, way).wait_recv()
        pass_on(slot, way)

    def sent(slot, way):
        @pl.when(l > 0 if way else l < NL - 1)
        def _():
            chain_copy(slot, way).wait_send()

    for k in range(len(pieces)):
        q, first, _ = pieces[k]
        if k == 1:
            pass_on(l, 0)
            pass_on(l, 1)
            on_chain(1, relay)
            finish_weights()
            on_chain(2, relay)
        for dz in range(2):
            def step(dx, _, dz=dz, q=q, k=k, first=first):
                h = mod(x + dx, NX) * 2 + mod(lax.div(z, 2) + dz, 2)
                if first == 0:
                    for i in range(4):
                        src = 4 * h + i

                        @pl.when(src != me)
                        def _():
                            return_copy(q, src, src).wait_recv()

                blend(k, h)
                return 0

            lax.fori_loop(0, NX, step, 0)
    share_weights()

    def gathered(k):
        for d in (1, 3, 2):
            def step(h, _, d=d):
                mix_copy(d, k, h, mod(l - d + NL, NL)).wait()
                return 0

            lax.fori_loop(0, SEQ // 4, step, 0)

    def product(o, k):
        q, first, last = pieces[k]
        t = mod(x - o + NX, NX)
        left = jnp.concatenate([weight[q, t, b] for b in range(NL)], 1)
        half = BLOCK // PARTS
        right = mix[:, half * q:half * (q + 1), LANES * first:LANES * last]
        return jnp.dot(left, right.reshape(NL * half, LANES * (last - first)), preferred_element_type=F32)

    def partial_copy(d, k):
        return remote(psend.at[d - 1, k - 1], pgot.at[d - 1, k - 1], pssem.at[d - 1, k - 1],
                      prsem.at[d - 1, k - 1], me, mod(y + d, NY) * NL + l)

    for t in range(NX):
        core_copy(t, 1 - c).wait()
    on_chain(3, lambda slot, way: chain_copy(slot, way).wait_recv())
    sent(l, 0)
    sent(l, 1)
    on_chain(1, sent)
    on_chain(2, sent)
    for d in range(NY):
        acc[d] = product(mod(y + d, NY), 0)
    for k in (1, 2):
        cols = slice(LANES * pieces[k][1], LANES * pieces[k][2])
        gathered(k)
        for d in (2, 1, 3):
            psend[d - 1, k - 1] = (acc[d, :, cols] + product(mod(y + d, NY), k)).astype(BF16)
            partial_copy(d, k).start()
        acc[0, :, cols] += product(y, k)
    for q in range(PARTS):
        each_partner(lambda to: scatter_copy(q, to, me).wait_send())
        each_partner(lambda to: return_copy(q, to, me).wait_send())
    for k in (1, 2):
        cols = slice(LANES * pieces[k][1], LANES * pieces[k][2])
        total = acc[0, :, cols]
        for d in (1, 3, 2):
            partial_copy(d, k).wait()
            total = total + pgot[d - 1, k - 1].astype(F32)
        o_ref[:, cols] = total.astype(BF16)


def per_device(values, gates, skip_gain, filters, out_weight):
    dma = pltpu.SemaphoreType.DMA
    hbm = pl.BlockSpec(memory_space=pltpu.HBM)
    vmem = pl.BlockSpec(memory_space=VMEM)
    return pl.pallas_call(
        block_kernel,
        out_shape=jax.ShapeDtypeStruct((BLOCK, TOKENS), BF16),
        in_specs=[hbm, hbm, hbm, hbm, hbm],
        out_specs=vmem,
        scratch_shapes=[
            VMEM((BLOCK, TOKENS), BF16), VMEM((BLOCK, TOKENS), BF16), VMEM((BLOCK, TOKENS), BF16),
            VMEM((1, BLOCK), F32), VMEM((LANES, BLOCK), BF16), VMEM((BLOCK, LANES), F32),
            VMEM((PARTS, SEQ, 2 * BOX, LANES), BF16), VMEM((PARTS, SEQ, 2 * BOX, LANES), BF16),
            VMEM((COUNT * CH + LANES, LANES), F32), VMEM((COUNT * CH + CH, LANES), F32),
            VMEM((COUNT * CH, LANES), F32),
            VMEM((2, COUNT, 4 * LANES), BF16), VMEM((2, 4 * LANES, 2 * LANES), BF16),
            VMEM((2, COUNT, 2 * LANES), F32),
            VMEM((PARTS, SEQ, BOX, LANES), BF16), VMEM((PARTS, SEQ, BOX, LANES), BF16),
            VMEM((NL, BLOCK, TOKENS), BF16),
            VMEM((NZ, BLOCK, LANES), BF16), VMEM((NC, NX, NZ, BLOCK, LANES), BF16),
            VMEM((NY, BLOCK, TOKENS), F32),
            VMEM((3, 2, BLOCK, TOKENS // 2), BF16), VMEM((3, 2, BLOCK, TOKENS // 2), BF16),
            dma((5,)), dma((PARTS, SEQ)), dma((PARTS, SEQ)), dma((PARTS, SEQ)), dma((PARTS, SEQ)),
            dma((4,)), dma((4,)), dma((NZ, NX)), dma((NZ, NX)), dma((NX,)), dma((NX,)),
            dma((3, SEQ // 2)), dma((3, SEQ // 2)), dma((NL, 2)), dma((NL,)), dma((3, 2)), dma((3, 2)),
        ],
        compiler_params=pltpu.CompilerParams(
            collective_id=1, has_side_effects=True, vmem_limit_bytes=64 * 2**20),
        name="hyena_block",
    )(values, filters, gates, skip_gain[None], out_weight)


def solution(mesh):
    return jax.shard_map(
        per_device,
        mesh=mesh,
        in_specs=(
            P("chan", "seq"),
            P("chan", "seq"),
            P("chan"),
            P("chan", "seq"),
            P("seq", "chan"),
        ),
        out_specs=P("chan", "seq"),
        check_vma=False,
    )
```

time: 121 us -> 103 us (0.85)
  the two profiles are of different devices: /device:TPU:33 before, /device:TPU:6 now
where the time goes in v2:
time: 103 us; the launch traced here: 102 us
  Pallas kernels  101 us (98%)
  local copies, waits for them, and re-layouts  1.67 us (2%)
    pallas_call x1, Pallas kernels, per_device(): pl.pallas_call(block_kernel, out_shape=jax.ShapeDtypeStruct((BLOCK, TOKEN...  101 us

profile of v2, /device:TPU:6, one launch (start us, length us, event | category | flops | bytes accessed | tf_op | source)
XLA Modules:
  0.0 102.4 jit_solution(6431947981463308066)
XLA Ops:
  0.0 100.7 %hyena_block.1 = bf16[256,512]{1,0:T(8,128)(2,1)} custom-call(bf16[256,512]{1,0:T(8,128)(2,1)} %v_hbm.1, bf16[256,512]{1,0:T(8,128)(2,1)} %f_hbm.1, bf16[256,512]{1,0:T(8,128)(2,1)} %g_hbm.1, f32[1,256]{1,0:T(1,128)} %bitcast.1, bf16[128,256]{1,0:T(8,128)(2,1)} %w_hbm.1), custom_call_target="tpu_custom_call" | custom-call | tf_op jit(solution)/shard_map/hyena_block/pallas_call | solution.py:382
  100.7 1.7 %copy.7 = bf16[256,512]{1,0:T(8,128)(2,1)} copy(bf16[256,512]{1,0:T(8,128)(2,1)} %hyena_block.1) | data formatting | bytes 524288

commit v3 on v2

--- a/solution.py
+++ b/solution.py
@@ -218,8 +218,6 @@
     each_partner(lambda to: scatter_copy(0, to, me).start())
     pack(1)
     each_partner(lambda to: scatter_copy(1, to, me).start())
-    weight_copy(0, z).start()
-    weight_copy(1, z).start()
     send_across(z)
     got[0, me] = out[0, me]
     got[1, me] = out[1, me]
@@ -232,6 +230,9 @@
     for q in range(PARTS):
         each_partner(lambda to: scatter_copy(q, to, to).wait_recv())
         if q == 0:
+            weight_copy(0, z).start()
+            weight_copy(1, z).start()
+        else:
             relay_weights()
 
         def load(q=q):

time: 103 us -> 98.6 us (0.957)
  Pallas kernels: 101 us -> 96.2 us
    pallas_call x1, Pallas kernels: 101 us -> 96.2 us  [per_device(): pl.pallas_call(block_kernel, out_shape=jax.ShapeDtypeStruct((BLOCK, TOKEN...]
where the time goes in v3:
time: 98.6 us; the launch traced here: 97.9 us
  Pallas kernels  96.2 us (98%)
  local copies, waits for them, and re-layouts  1.67 us (2%)
    pallas_call x1, Pallas kernels, per_device(): pl.pallas_call(block_kernel, out_shape=jax.ShapeDtypeStruct((BLOCK, TOKEN...  96.2 us

profile of v3, /device:TPU:6, one launch (start us, length us, event | category | flops | bytes accessed | tf_op | source)
XLA Modules:
  0.0 97.9 jit_solution(14111131090401762466)
XLA Ops:
  0.0 96.2 %hyena_block.1 = bf16[256,512]{1,0:T(8,128)(2,1)} custom-call(bf16[256,512]{1,0:T(8,128)(2,1)} %v_hbm.1, bf16[256,512]{1,0:T(8,128)(2,1)} %f_hbm.1, bf16[256,512]{1,0:T(8,128)(2,1)} %g_hbm.1, f32[1,256]{1,0:T(1,128)} %bitcast.1, bf16[128,256]{1,0:T(8,128)(2,1)} %w_hbm.1), custom_call_target="tpu_custom_call" | custom-call | tf_op jit(solution)/shard_map/hyena_block/pallas_call | solution.py:383
  96.2 1.7 %copy.7 = bf16[256,512]{1,0:T(8,128)(2,1)} copy(bf16[256,512]{1,0:T(8,128)(2,1)} %hyena_block.1) | data formatting | bytes 524288

commit v4 on v3

--- a/solution.py
+++ b/solution.py
@@ -232,8 +232,6 @@
         if q == 0:
             weight_copy(0, z).start()
             weight_copy(1, z).start()
-        else:
-            relay_weights()
 
         def load(q=q):
             vf[LANES:, :] = got[q, :, 0:BOX, :].astype(F32).reshape(COUNT * CH, LANES)
@@ -243,6 +241,8 @@
         done[q] = yf[...].astype(BF16).reshape(SEQ, BOX, LANES)
         each_partner(lambda to: return_copy(q, to, me).start())
         back[q, me] = done[q, me]
+
+    relay_weights()
 
     pieces = ((0, 0, ROWS), (1, 0, ROWS // 2), (1, ROWS // 2, ROWS))
 

time: 98.6 us -> 99.2 us (level)
  no operation moved by 1% of the time
where the time goes in v4:
time: 99.2 us; the launch traced here: 97.9 us
  Pallas kernels  96.2 us (97%)
  local copies, waits for them, and re-layouts  1.67 us (2%)
    pallas_call x1, Pallas kernels, per_device(): pl.pallas_call(block_kernel, out_shape=jax.ShapeDtypeStruct((BLOCK, TOKEN...  96.2 us

profile of v4, /device:TPU:6, one launch (start us, length us, event | category | flops | bytes accessed | tf_op | source)
XLA Modules:
  0.0 97.9 jit_solution(2243028450324482611)
XLA Ops:
  0.0 96.2 %hyena_block.1 = bf16[256,512]{1,0:T(8,128)(2,1)} custom-call(bf16[256,512]{1,0:T(8,128)(2,1)} %v_hbm.1, bf16[256,512]{1,0:T(8,128)(2,1)} %f_hbm.1, bf16[256,512]{1,0:T(8,128)(2,1)} %g_hbm.1, f32[1,256]{1,0:T(1,128)} %bitcast.1, bf16[128,256]{1,0:T(8,128)(2,1)} %w_hbm.1), custom_call_target="tpu_custom_call" | custom-call | tf_op jit(solution)/shard_map/hyena_block/pallas_call | solution.py:383
  96.2 1.7 %copy.7 = bf16[256,512]{1,0:T(8,128)(2,1)} copy(bf16[256,512]{1,0:T(8,128)(2,1)} %hyena_block.1) | data formatting | bytes 524288
